TPU v7x, 256 devices: a whole 4x4x8 slice. The times are simulated.
256 devices in a mesh: segment: 4 (over y_hi, core), frame: 64 (over x, z, y_lo).
Axes of the slice: x: 4, y: 4 (y_hi: 2, y_lo: 2; y = y_hi * 2 + y_lo), z: 8, core: 2. Of those that a mesh axis runs over, the one named last changes fastest.
Arguments:
- clips: bfloat16 [4, 64, 320, 1024], P('segment', 'frame'), may hold values from -6 to 6
- timesteps: int32 [4], replicated, may hold values from 0 to 999
- gain: float32 [4, 320], replicated, may hold values from 0.25 to 1.75
- temporal_weight: bfloat16 [4, 3, 320, 320], P('segment'), may hold values from -0.1875 to 0.1875
- film_weight: bfloat16 [4, 320, 320], P('segment'), may hold values from -0.3125 to 0.3125
- out_weight: bfloat16 [4, 320, 320], P('segment'), may hold values from -0.3125 to 0.3125
- skip_weight: bfloat16 [2, 320, 320], replicated, may hold values from -0.3125 to 0.3125
Outputs:
- video_out: bfloat16 [4, 64, 320, 1024], P('segment', 'frame')
All inputs are finite; a program needn't handle non-finite values.
Results may differ from a plain program's by a relative error of at most 0.012.
Values may be sent and summed in bfloat16 or wider, within the bound.
A program may use at most 64 MiB of HBM per device.

v0:
```python
import math
import jax
import jax.numpy as jnp
from jax import lax
from jax.sharding import PartitionSpec as P


def extended(cells, sides, width):
    for axis, dim in sides:
        count = lax.axis_size(axis)
        ends = count - 1
        head = lax.slice_in_dim(cells, 0, width, axis=dim)
        tail = lax.slice_in_dim(cells, cells.shape[dim] - width, cells.shape[dim], axis=dim)
        cells = jnp.concatenate(
            [
                lax.ppermute(tail, axis, [(i, (i + 1) % count) for i in range(ends)]),
                cells,
                lax.ppermute(head, axis, [((i + 1) % count, i) for i in range(ends)]),
            ],
            axis=dim,
        )
    return cells


def shifted(array, axis, by):
    length = lax.axis_size(axis)
    pairs = [(i, i + by) for i in range(length) if 0 <= i + by < length]
    return lax.ppermute(array, axis, pairs)


def embed(timesteps, width):
    half = width // 2
    freq = jnp.exp(-math.log(10000.0) * jnp.arange(half, dtype=jnp.float32) / half)
    angle = timesteps.astype(jnp.float32)[:, None] * freq[None, :]
    return jnp.concatenate([jnp.sin(angle), jnp.cos(angle)], axis=-1).astype(jnp.bfloat16)


def channel_mix(weight, field):
    return jnp.einsum("io,fip->fop", weight, field, preferred_element_type=jnp.float32)


def temporal_mix(normed, taps):
    padded = extended(normed, (("frame", 0),), 1)
    count = normed.shape[0]
    mixed = channel_mix(taps[0], padded[0:count])
    mixed = mixed + channel_mix(taps[1], padded[1 : count + 1])
    mixed = mixed + channel_mix(taps[2], padded[2 : count + 2])
    return mixed


def section_core(state, own_gain, taps, film_vec, projection):
    values = state.astype(jnp.float32)
    meansq = jnp.mean(values * values, axis=1, keepdims=True)
    normed = (values * lax.rsqrt(meansq + 1e-05) * own_gain[None, :, None]).astype(jnp.bfloat16)
    mixed = temporal_mix(normed, taps)
    hidden = jax.nn.silu(mixed * (1.0 + film_vec[None, :, None])).astype(jnp.bfloat16)
    return values + channel_mix(projection, hidden)


def shards(clips, timesteps, gain, temporal_weight, film_weight, out_weight, skip_weight):
    sections = lax.axis_size("segment")
    section = lax.axis_index("segment")
    emb = embed(timesteps, clips.shape[2])
    all_clips = lax.all_gather(clips, "segment", axis=0, tiled=True)
    batches = all_clips.shape[0]
    film_all = jnp.dot(emb, film_weight[0], preferred_element_type=jnp.float32)
    own_gain = lax.dynamic_index_in_dim(gain, section, 0, keepdims=False)
    taps = temporal_weight[0]
    projection = out_weight[0]
    decoder_weight = jnp.where(section == sections - 1, skip_weight[1], skip_weight[0])
    is_first = section == 0
    is_decoder = section >= 2
    empty = jnp.zeros(all_clips.shape[1:], jnp.bfloat16)
    handed = empty
    carried = empty
    finals = []
    steps_total = batches + sections - 1
    for step in range(steps_total):
        source = all_clips[step] if step < batches else empty
        state = jnp.where(is_first, source, handed)
        micro = step - section
        select = jnp.arange(batches) == micro
        film_vec = jnp.sum(jnp.where(select[:, None], film_all, 0.0), axis=0)
        far_skip = empty
        if step >= 3 and step - 3 < batches:
            far_skip = all_clips[step - 3]
        skip_in = jnp.where(section == sections - 1, far_skip, carried)
        total = section_core(state, own_gain, taps, film_vec, projection)
        skip_term = channel_mix(decoder_weight, skip_in)
        total = total + jnp.where(is_decoder, skip_term, 0.0)
        result = total.astype(jnp.bfloat16)
        if step >= sections - 1:
            finals.append(result)
        if step < steps_total - 1:
            handed, carried = shifted((result, state), "segment", 1)
    stacked = jnp.stack(finals, axis=0).astype(jnp.float32)
    stacked = jnp.where(section == sections - 1, stacked, 0.0)
    return lax.psum_scatter(
        stacked.astype(jnp.bfloat16), "segment", scatter_dimension=0, tiled=True
    )


def solution(mesh):
    placed = (
        P("segment", "frame", None, None),
        P(),
        P(),
        P("segment", None, None, None),
        P("segment", None, None),
        P("segment", None, None),
        P(),
    )
    return jax.shard_map(
        shards,
        mesh=mesh,
        in_specs=placed,
        out_specs=P("segment", "frame", None, None),
        check_vma=False,
    )
```

profile of v0, /device:TPU:1, one launch (start us, length us, event | category | flops | bytes accessed | tf_op | source)
XLA Modules:
  0.0 453.3 jit_solution(10235497476458363797)
XLA Ops:
  10.0 35.6 %all-gather.2.cloned.1.call-done = bf16[4,1,320,1024]{3,2,1,0:T(8,128)(2,1)} async-done(((bf16[1,1,320,1024]{3,2,1,0:T(8,128)(2,1)}), bf16[4,1,320,1024]{3,2,1,0:T(8,128)(2,1)}) %all-gather.2.cloned.1.call-update) | async-done | bytes 2621456 | tf_op jit(solution)/shard_map/all_gather | solution.py:64
  48.7 4.9 %collective-permute-start = (bf16[1,320,1024]{2,1,0:T(8,128)(2,1)S(1)}, bf16[1,320,1024]{2,1,0:T(8,128)(2,1)}, u32[]{:S(2)}, u32[]{:S(2)}) collective-permute-start(bf16[1,320,1024]{2,1,0:T(8,128)(2,1)S(1)} %fusion.51), channel_id=1, source_target_pairs={{0,1},{1,2},{2,3},{3,4},{4,5},{5,6},{6,7},{7,8},{8,9},{9,10},{10,1... | collective-permute-start | bytes 1966088 | tf_op jit(solution)/shard_map/ppermute | solution.py:16
  56.3 8.7 %collective-permute-done.1 = bf16[1,320,1024]{2,1,0:T(8,128)(2,1)S(1)} collective-permute-done((bf16[1,320,1024]{2,1,0:T(8,128)(2,1)S(1)}, bf16[1,320,1024]{2,1,0:T(8,128)(2,1)S(1)}, u32[]{:S(2)}, u32[]{:S(2)}) %collective-permute-start.1) | collective-permute-done | bytes 655392 | tf_op jit(solution)/shard_map/ppermute | solution.py:18
  66.7 12.0 %collective-permute-done = bf16[1,320,1024]{2,1,0:T(8,128)(2,1)} collective-permute-done((bf16[1,320,1024]{2,1,0:T(8,128)(2,1)S(1)}, bf16[1,320,1024]{2,1,0:T(8,128)(2,1)}, u32[]{:S(2)}, u32[]{:S(2)}) %collective-permute-start) | collective-permute-done | bytes 655392 | tf_op jit(solution)/shard_map/ppermute | solution.py:16
  82.2 4.0 collective-permute-start.2
  88.2 5.5 %collective-permute-done.2 = bf16[1,320,1024]{2,1,0:T(8,128)(2,1)S(1)} collective-permute-done((bf16[1,320,1024]{2,1,0:T(8,128)(2,1)S(1)}, bf16[1,320,1024]{2,1,0:T(8,128)(2,1)S(1)}, u32[]{:S(2)}, u32[]{:S(2)}) %collective-permute-start.2) | collective-permute-done | bytes 655392 | tf_op jit(solution)/shard_map/ppermute | solution.py:28
  96.7 5.9 %collective-permute-start.3 = (bf16[1,320,1024]{2,1,0:T(8,128)(2,1)S(1)}, bf16[1,320,1024]{2,1,0:T(8,128)(2,1)}, u32[]{:S(2)}, u32[]{:S(2)}) collective-permute-start(bf16[1,320,1024]{2,1,0:T(8,128)(2,1)S(1)} %fusion.54), channel_id=1, source_target_pairs={{0,1},{1,2},{2,3},{3,4},{4,5},{5,6},{6,7},{7,8},{8,9},{9,10},{10,1... | collective-permute-start | bytes 1966088 | tf_op jit(solution)/shard_map/ppermute | solution.py:16
  102.5 17.2 %collective-permute-done.5 = bf16[1,320,1024]{2,1,0:T(8,128)(2,1)S(1)} collective-permute-done((bf16[1,320,1024]{2,1,0:T(8,128)(2,1)S(1)}, bf16[1,320,1024]{2,1,0:T(8,128)(2,1)S(1)}, u32[]{:S(2)}, u32[]{:S(2)}) %collective-permute-start.5) | collective-permute-done | bytes 655392 | tf_op jit(solution)/shard_map/ppermute | solution.py:28
  124.7 4.2 collective-permute-done.3
  136.2 5.6 %collective-permute-done.6 = bf16[1,320,1024]{2,1,0:T(8,128)(2,1)S(1)} collective-permute-done((bf16[1,320,1024]{2,1,0:T(8,128)(2,1)S(1)}, bf16[1,320,1024]{2,1,0:T(8,128)(2,1)S(1)}, u32[]{:S(2)}, u32[]{:S(2)}) %collective-permute-start.6) | collective-permute-done | bytes 655392 | tf_op jit(solution)/shard_map/ppermute | solution.py:28
  144.7 6.2 %collective-permute-start.7 = (bf16[1,320,1024]{2,1,0:T(8,128)(2,1)S(1)}, bf16[1,320,1024]{2,1,0:T(8,128)(2,1)}, u32[]{:S(2)}, u32[]{:S(2)}) collective-permute-start(bf16[1,320,1024]{2,1,0:T(8,128)(2,1)S(1)} %fusion.57), channel_id=1, source_target_pairs={{0,1},{1,2},{2,3},{3,4},{4,5},{5,6},{6,7},{7,8},{8,9},{9,10},{10,1... | collective-permute-start | bytes 1966088 | tf_op jit(solution)/shard_map/ppermute | solution.py:16
  150.9 15.6 %collective-permute-done.9 = bf16[1,320,1024]{2,1,0:T(8,128)(2,1)S(1)} collective-permute-done((bf16[1,320,1024]{2,1,0:T(8,128)(2,1)S(1)}, bf16[1,320,1024]{2,1,0:T(8,128)(2,1)S(1)}, u32[]{:S(2)}, u32[]{:S(2)}) %collective-permute-start.9) | collective-permute-done | bytes 655392 | tf_op jit(solution)/shard_map/ppermute | solution.py:28
  170.3 6.6 %collective-permute-done.7 = bf16[1,320,1024]{2,1,0:T(8,128)(2,1)} collective-permute-done((bf16[1,320,1024]{2,1,0:T(8,128)(2,1)S(1)}, bf16[1,320,1024]{2,1,0:T(8,128)(2,1)}, u32[]{:S(2)}, u32[]{:S(2)}) %collective-permute-start.7) | collective-permute-done | bytes 655392 | tf_op jit(solution)/shard_map/ppermute | solution.py:16
  176.9 3.9 fusion.46
  184.7 5.9 %collective-permute-done.10 = bf16[1,320,1024]{2,1,0:T(8,128)(2,1)S(1)} collective-permute-done((bf16[1,320,1024]{2,1,0:T(8,128)(2,1)}, bf16[1,320,1024]{2,1,0:T(8,128)(2,1)S(1)}, u32[]{:S(2)}, u32[]{:S(2)}) %collective-permute-start.10) | collective-permute-done | bytes 655392 | tf_op jit(solution)/shard_map/ppermute | solution.py:28
  193.4 6.4 %collective-permute-start.11 = (bf16[1,320,1024]{2,1,0:T(8,128)(2,1)S(1)}, bf16[1,320,1024]{2,1,0:T(8,128)(2,1)}, u32[]{:S(2)}, u32[]{:S(2)}) collective-permute-start(bf16[1,320,1024]{2,1,0:T(8,128)(2,1)S(1)} %fusion.60), channel_id=1, source_target_pairs={{0,1},{1,2},{2,3},{3,4},{4,5},{5,6},{6,7},{7,8},{8,9},{9,10},{10,1... | collective-permute-start | bytes 1966088 | tf_op jit(solution)/shard_map/ppermute | solution.py:16
  199.8 15.5 %collective-permute-done.13 = bf16[1,320,1024]{2,1,0:T(8,128)(2,1)S(1)} collective-permute-done((bf16[1,320,1024]{2,1,0:T(8,128)(2,1)S(1)}, bf16[1,320,1024]{2,1,0:T(8,128)(2,1)S(1)}, u32[]{:S(2)}, u32[]{:S(2)}) %collective-permute-start.13) | collective-permute-done | bytes 655392 | tf_op jit(solution)/shard_map/ppermute | solution.py:28
  221.4 4.2 collective-permute-done.11
  232.9 5.6 %collective-permute-done.14 = bf16[1,320,1024]{2,1,0:T(8,128)(2,1)S(1)} collective-permute-done((bf16[1,320,1024]{2,1,0:T(8,128)(2,1)S(1)}, bf16[1,320,1024]{2,1,0:T(8,128)(2,1)S(1)}, u32[]{:S(2)}, u32[]{:S(2)}) %collective-permute-start.14) | collective-permute-done | bytes 655392 | tf_op jit(solution)/shard_map/ppermute | solution.py:28
  240.2 7.3 %collective-permute-start.15 = (bf16[1,320,1024]{2,1,0:T(8,128)(2,1)S(1)}, bf16[1,320,1024]{2,1,0:T(8,128)(2,1)}, u32[]{:S(2)}, u32[]{:S(2)}) collective-permute-start(bf16[1,320,1024]{2,1,0:T(8,128)(2,1)S(1)} %fusion.63), channel_id=1, source_target_pairs={{0,1},{1,2},{2,3},{3,4},{4,5},{5,6},{6,7},{7,8},{8,9},{9,10},{10,1... | collective-permute-start | bytes 1966088 | tf_op jit(solution)/shard_map/ppermute | solution.py:16
  247.5 9.7 %collective-permute-done.17 = bf16[1,320,1024]{2,1,0:T(8,128)(2,1)S(1)} collective-permute-done((bf16[1,320,1024]{2,1,0:T(8,128)(2,1)S(1)}, bf16[1,320,1024]{2,1,0:T(8,128)(2,1)S(1)}, u32[]{:S(2)}, u32[]{:S(2)}) %collective-permute-start.17) | collective-permute-done | bytes 655392 | tf_op jit(solution)/shard_map/ppermute | solution.py:28
  263.6 10.0 %collective-permute-done.15 = bf16[1,320,1024]{2,1,0:T(8,128)(2,1)} collective-permute-done((bf16[1,320,1024]{2,1,0:T(8,128)(2,1)S(1)}, bf16[1,320,1024]{2,1,0:T(8,128)(2,1)}, u32[]{:S(2)}, u32[]{:S(2)}) %collective-permute-start.15) | collective-permute-done | bytes 655392 | tf_op jit(solution)/shard_map/ppermute | solution.py:16
  273.6 3.9 fusion.44
  281.3 5.9 %collective-permute-done.18 = bf16[1,320,1024]{2,1,0:T(8,128)(2,1)S(1)} collective-permute-done((bf16[1,320,1024]{2,1,0:T(8,128)(2,1)}, bf16[1,320,1024]{2,1,0:T(8,128)(2,1)S(1)}, u32[]{:S(2)}, u32[]{:S(2)}) %collective-permute-start.18) | collective-permute-done | bytes 655392 | tf_op jit(solution)/shard_map/ppermute | solution.py:28
  289.0 11.8 %collective-permute-start.19 = (bf16[1,320,1024]{2,1,0:T(8,128)(2,1)S(1)}, bf16[1,320,1024]{2,1,0:T(8,128)(2,1)}, u32[]{:S(2)}, u32[]{:S(2)}) collective-permute-start(bf16[1,320,1024]{2,1,0:T(8,128)(2,1)S(1)} %fusion.66), channel_id=1, source_target_pairs={{0,1},{1,2},{2,3},{3,4},{4,5},{5,6},{6,7},{7,8},{8,9},{9,10},{10,1... | collective-permute-start | bytes 1966088 | tf_op jit(solution)/shard_map/ppermute | solution.py:16
  305.1 9.7 %collective-permute-done.20 = bf16[1,320,1024]{2,1,0:T(8,128)(2,1)S(1)} collective-permute-done((bf16[1,320,1024]{2,1,0:T(8,128)(2,1)S(1)}, bf16[1,320,1024]{2,1,0:T(8,128)(2,1)S(1)}, u32[]{:S(2)}, u32[]{:S(2)}) %collective-permute-start.20) | collective-permute-done | bytes 655392 | tf_op jit(solution)/shard_map/ppermute | solution.py:18
  323.8 10.7 %collective-permute-done.22 = bf16[1,320,1024]{2,1,0:T(8,128)(2,1)S(1)} collective-permute-done((bf16[1,320,1024]{2,1,0:T(8,128)(2,1)S(1)}, bf16[1,320,1024]{2,1,0:T(8,128)(2,1)S(1)}, u32[]{:S(2)}, u32[]{:S(2)}) %collective-permute-start.22) | collective-permute-done | bytes 655392 | tf_op jit(solution)/shard_map/ppermute | solution.py:28
  336.2 18.9 %collective-permute-start.23 = (bf16[1,320,1024]{2,1,0:T(8,128)(2,1)S(1)}, bf16[1,320,1024]{2,1,0:T(8,128)(2,1)}, u32[]{:S(2)}, u32[]{:S(2)}) collective-permute-start(bf16[1,320,1024]{2,1,0:T(8,128)(2,1)S(1)} %fusion.69), channel_id=1, source_target_pairs={{0,1},{1,2},{2,3},{3,4},{4,5},{5,6},{6,7},{7,8},{8,9},{9,10},{10,1... | collective-permute-start | bytes 1966088 | tf_op jit(solution)/shard_map/ppermute | solution.py:16
  358.4 11.1 %collective-permute-done.24 = bf16[1,320,1024]{2,1,0:T(8,128)(2,1)S(1)} collective-permute-done((bf16[1,320,1024]{2,1,0:T(8,128)(2,1)S(1)}, bf16[1,320,1024]{2,1,0:T(8,128)(2,1)S(1)}, u32[]{:S(2)}, u32[]{:S(2)}) %collective-permute-start.24) | collective-permute-done | bytes 655392 | tf_op jit(solution)/shard_map/ppermute | solution.py:18
  371.2 5.2 %collective-permute-done.23 = bf16[1,320,1024]{2,1,0:T(8,128)(2,1)} collective-permute-done((bf16[1,320,1024]{2,1,0:T(8,128)(2,1)S(1)}, bf16[1,320,1024]{2,1,0:T(8,128)(2,1)}, u32[]{:S(2)}, u32[]{:S(2)}) %collective-permute-start.23) | collective-permute-done | bytes 655392 | tf_op jit(solution)/shard_map/ppermute | solution.py:16
  376.3 3.9 fusion.72
  383.3 63.1 %reduce-scatter.2.cloned.1.call-done = bf16[1,1,320,1024]{3,2,1,0:T(8,128)(2,1)} async-done(((bf16[4,1,320,1024]{3,2,1,0:T(8,128)(2,1)}), bf16[1,1,320,1024]{3,2,1,0:T(8,128)(2,1)}) %reduce-scatter.2.cloned.1.call-update) | async-done | bytes 655376 | tf_op jit(solution)/shard_map/reduce_scatter | solution.py:98
  (103 shorter events, 94.7 us)
Async XLA Ops:
  6.5 72.2 %copy-start = (bf16[1,320,320]{2,1,0:T(8,128)(2,1)S(1)}, bf16[1,320,320]{2,1,0:T(8,128)(2,1)}, u32[]{:S(2)}) copy-start(bf16[1,320,320]{2,1,0:T(8,128)(2,1)} %param.12) | copy-start | bytes 614404
  6.5 39.0 %all-gather.2.cloned.1.call-start = ((), (), s32[]{:S(2)}) async-start(), calls=%async_computation.1 | async-start | bytes 3276800 | tf_op jit(solution)/shard_map/all_gather | solution.py:64
  7.3 439.2 %reduce-scatter.2.cloned.1.call-start = ((), (), s32[]{:S(2)}) async-start(), calls=%async_computation.2 | async-start | bytes 3276800 | tf_op jit(solution)/shard_map/reduce_scatter | solution.py:98
  10.0 38.4 %copy-start.4 = (bf16[1,320,320]{2,1,0:T(8,128)(2,1)S(1)}, bf16[1,320,320]{2,1,0:T(8,128)(2,1)}, u32[]{:S(2)}) copy-start(bf16[1,320,320]{2,1,0:T(8,128)(2,1)} %param.11) | copy-start | bytes 614404
  10.0 43.5 %copy-start.1 = (bf16[1,3,320,320]{3,2,1,0:T(8,128)(2,1)S(1)}, bf16[1,3,320,320]{3,2,1,0:T(8,128)(2,1)}, u32[]{:S(2)}) copy-start(bf16[1,3,320,320]{3,2,1,0:T(8,128)(2,1)} %param.10) | copy-start | bytes 1843204
  47.1 18.0 %collective-permute-start.1 = (bf16[1,320,1024]{2,1,0:T(8,128)(2,1)S(1)}, bf16[1,320,1024]{2,1,0:T(8,128)(2,1)S(1)}, u32[]{:S(2)}, u32[]{:S(2)}) collective-permute-start(bf16[1,320,1024]{2,1,0:T(8,128)(2,1)S(1)} %fusion.51), channel_id=1, source_target_pairs={{1,0},{2,1},{3,2},{4,3},{5,4},{6,5},{7,6},{8,7},{9,8},{10,9},{11,1... | collective-permute-start | bytes 1966088 | tf_op jit(solution)/shard_map/ppermute | solution.py:18
  48.7 30.0 %collective-permute-start = (bf16[1,320,1024]{2,1,0:T(8,128)(2,1)S(1)}, bf16[1,320,1024]{2,1,0:T(8,128)(2,1)}, u32[]{:S(2)}, u32[]{:S(2)}) collective-permute-start(bf16[1,320,1024]{2,1,0:T(8,128)(2,1)S(1)} %fusion.51), channel_id=1, source_target_pairs={{0,1},{1,2},{2,3},{3,4},{4,5},{5,6},{6,7},{7,8},{8,9},{9,10},{10,1... | collective-permute-start | bytes 1966088 | tf_op jit(solution)/shard_map/ppermute | solution.py:16
  82.2 11.5 %collective-permute-start.2 = (bf16[1,320,1024]{2,1,0:T(8,128)(2,1)S(1)}, bf16[1,320,1024]{2,1,0:T(8,128)(2,1)S(1)}, u32[]{:S(2)}, u32[]{:S(2)}) collective-permute-start(bf16[1,320,1024]{2,1,0:T(8,128)(2,1)S(1)} %fusion.48), channel_id=1, source_target_pairs={{0,64},{64,128},{128,192},{1,65},{65,129},{129,193},{2,66},{66,130... | collective-permute-start | bytes 1966088 | tf_op jit(solution)/shard_map/ppermute | solution.py:28
  86.3 33.4 %collective-permute-start.5 = (bf16[1,320,1024]{2,1,0:T(8,128)(2,1)S(1)}, bf16[1,320,1024]{2,1,0:T(8,128)(2,1)S(1)}, u32[]{:S(2)}, u32[]{:S(2)}) collective-permute-start(bf16[1,320,1024]{2,1,0:T(8,128)(2,1)S(1)} %get-tuple-element.23), channel_id=1, source_target_pairs={{0,64},{64,128},{128,192},{1,65},{65,129},{129,193},{2,66},{66,130... | collective-permute-start | bytes 1966088 | tf_op jit(solution)/shard_map/ppermute | solution.py:28
  95.4 27.7 %collective-permute-start.4 = (bf16[1,320,1024]{2,1,0:T(8,128)(2,1)S(1)}, bf16[1,320,1024]{2,1,0:T(8,128)(2,1)S(1)}, u32[]{:S(2)}, u32[]{:S(2)}) collective-permute-start(bf16[1,320,1024]{2,1,0:T(8,128)(2,1)S(1)} %fusion.54), channel_id=1, source_target_pairs={{1,0},{2,1},{3,2},{4,3},{5,4},{6,5},{7,6},{8,7},{9,8},{10,9},{11,1... | collective-permute-start | bytes 1966088 | tf_op jit(solution)/shard_map/ppermute | solution.py:18
  96.7 32.2 %collective-permute-start.3 = (bf16[1,320,1024]{2,1,0:T(8,128)(2,1)S(1)}, bf16[1,320,1024]{2,1,0:T(8,128)(2,1)}, u32[]{:S(2)}, u32[]{:S(2)}) collective-permute-start(bf16[1,320,1024]{2,1,0:T(8,128)(2,1)S(1)} %fusion.54), channel_id=1, source_target_pairs={{0,1},{1,2},{2,3},{3,4},{4,5},{5,6},{6,7},{7,8},{8,9},{9,10},{10,1... | collective-permute-start | bytes 1966088 | tf_op jit(solution)/shard_map/ppermute | solution.py:16
  132.4 9.4 %collective-permute-start.6 = (bf16[1,320,1024]{2,1,0:T(8,128)(2,1)S(1)}, bf16[1,320,1024]{2,1,0:T(8,128)(2,1)S(1)}, u32[]{:S(2)}, u32[]{:S(2)}) collective-permute-start(bf16[1,320,1024]{2,1,0:T(8,128)(2,1)S(1)} %fusion.47), channel_id=1, source_target_pairs={{0,64},{64,128},{128,192},{1,65},{65,129},{129,193},{2,66},{66,130... | collective-permute-start | bytes 1966088 | tf_op jit(solution)/shard_map/ppermute | solution.py:28
  134.3 32.2 %collective-permute-start.9 = (bf16[1,320,1024]{2,1,0:T(8,128)(2,1)S(1)}, bf16[1,320,1024]{2,1,0:T(8,128)(2,1)S(1)}, u32[]{:S(2)}, u32[]{:S(2)}) collective-permute-start(bf16[1,320,1024]{2,1,0:T(8,128)(2,1)S(1)} %get-tuple-element.21), channel_id=1, source_target_pairs={{0,64},{64,128},{128,192},{1,65},{65,129},{129,193},{2,66},{66,130... | collective-permute-start | bytes 1966088 | tf_op jit(solution)/shard_map/ppermute | solution.py:28
  143.4 25.3 %collective-permute-start.8 = (bf16[1,320,1024]{2,1,0:T(8,128)(2,1)S(1)}, bf16[1,320,1024]{2,1,0:T(8,128)(2,1)S(1)}, u32[]{:S(2)}, u32[]{:S(2)}) collective-permute-start(bf16[1,320,1024]{2,1,0:T(8,128)(2,1)S(1)} %fusion.57), channel_id=1, source_target_pairs={{1,0},{2,1},{3,2},{4,3},{5,4},{6,5},{7,6},{8,7},{9,8},{10,9},{11,1... | collective-permute-start | bytes 1966088 | tf_op jit(solution)/shard_map/ppermute | solution.py:18
  144.7 32.2 %collective-permute-start.7 = (bf16[1,320,1024]{2,1,0:T(8,128)(2,1)S(1)}, bf16[1,320,1024]{2,1,0:T(8,128)(2,1)}, u32[]{:S(2)}, u32[]{:S(2)}) collective-permute-start(bf16[1,320,1024]{2,1,0:T(8,128)(2,1)S(1)} %fusion.57), channel_id=1, source_target_pairs={{0,1},{1,2},{2,3},{3,4},{4,5},{5,6},{6,7},{7,8},{8,9},{9,10},{10,1... | collective-permute-start | bytes 1966088 | tf_op jit(solution)/shard_map/ppermute | solution.py:16
  180.8 9.7 %collective-permute-start.10 = (bf16[1,320,1024]{2,1,0:T(8,128)(2,1)}, bf16[1,320,1024]{2,1,0:T(8,128)(2,1)S(1)}, u32[]{:S(2)}, u32[]{:S(2)}) collective-permute-start(bf16[1,320,1024]{2,1,0:T(8,128)(2,1)} %fusion.46), channel_id=1, source_target_pairs={{0,64},{64,128},{128,192},{1,65},{65,129},{129,193},{2,66},{66,130... | collective-permute-start | bytes 1966088 | tf_op jit(solution)/shard_map/ppermute | solution.py:28
  182.7 32.6 %collective-permute-start.13 = (bf16[1,320,1024]{2,1,0:T(8,128)(2,1)S(1)}, bf16[1,320,1024]{2,1,0:T(8,128)(2,1)S(1)}, u32[]{:S(2)}, u32[]{:S(2)}) collective-permute-start(bf16[1,320,1024]{2,1,0:T(8,128)(2,1)S(1)} %get-tuple-element.19), channel_id=1, source_target_pairs={{0,64},{64,128},{128,192},{1,65},{65,129},{129,193},{2,66},{66,130... | collective-permute-start | bytes 1966088 | tf_op jit(solution)/shard_map/ppermute | solution.py:28
  192.1 27.6 %collective-permute-start.12 = (bf16[1,320,1024]{2,1,0:T(8,128)(2,1)S(1)}, bf16[1,320,1024]{2,1,0:T(8,128)(2,1)S(1)}, u32[]{:S(2)}, u32[]{:S(2)}) collective-permute-start(bf16[1,320,1024]{2,1,0:T(8,128)(2,1)S(1)} %fusion.60), channel_id=1, source_target_pairs={{1,0},{2,1},{3,2},{4,3},{5,4},{6,5},{7,6},{8,7},{9,8},{10,9},{11,1... | collective-permute-start | bytes 1966088 | tf_op jit(solution)/shard_map/ppermute | solution.py:18
  193.4 32.1 %collective-permute-start.11 = (bf16[1,320,1024]{2,1,0:T(8,128)(2,1)S(1)}, bf16[1,320,1024]{2,1,0:T(8,128)(2,1)}, u32[]{:S(2)}, u32[]{:S(2)}) collective-permute-start(bf16[1,320,1024]{2,1,0:T(8,128)(2,1)S(1)} %fusion.60), channel_id=1, source_target_pairs={{0,1},{1,2},{2,3},{3,4},{4,5},{5,6},{6,7},{7,8},{8,9},{9,10},{10,1... | collective-permute-start | bytes 1966088 | tf_op jit(solution)/shard_map/ppermute | solution.py:16
  229.0 9.4 %collective-permute-start.14 = (bf16[1,320,1024]{2,1,0:T(8,128)(2,1)S(1)}, bf16[1,320,1024]{2,1,0:T(8,128)(2,1)S(1)}, u32[]{:S(2)}, u32[]{:S(2)}) collective-permute-start(bf16[1,320,1024]{2,1,0:T(8,128)(2,1)S(1)} %fusion.45), channel_id=1, source_target_pairs={{0,64},{64,128},{128,192},{1,65},{65,129},{129,193},{2,66},{66,130... | collective-permute-start | bytes 1966088 | tf_op jit(solution)/shard_map/ppermute | solution.py:28
  231.0 26.3 %collective-permute-start.17 = (bf16[1,320,1024]{2,1,0:T(8,128)(2,1)S(1)}, bf16[1,320,1024]{2,1,0:T(8,128)(2,1)S(1)}, u32[]{:S(2)}, u32[]{:S(2)}) collective-permute-start(bf16[1,320,1024]{2,1,0:T(8,128)(2,1)S(1)} %get-tuple-element.17), channel_id=1, source_target_pairs={{0,64},{64,128},{128,192},{1,65},{65,129},{129,193},{2,66},{66,130... | collective-permute-start | bytes 1966088 | tf_op jit(solution)/shard_map/ppermute | solution.py:28
  238.9 23.1 %collective-permute-start.16 = (bf16[1,320,1024]{2,1,0:T(8,128)(2,1)S(1)}, bf16[1,320,1024]{2,1,0:T(8,128)(2,1)S(1)}, u32[]{:S(2)}, u32[]{:S(2)}) collective-permute-start(bf16[1,320,1024]{2,1,0:T(8,128)(2,1)S(1)} %fusion.63), channel_id=1, source_target_pairs={{1,0},{2,1},{3,2},{4,3},{5,4},{6,5},{7,6},{8,7},{9,8},{10,9},{11,1... | collective-permute-start | bytes 1966088 | tf_op jit(solution)/shard_map/ppermute | solution.py:18
  240.2 33.4 %collective-permute-start.15 = (bf16[1,320,1024]{2,1,0:T(8,128)(2,1)S(1)}, bf16[1,320,1024]{2,1,0:T(8,128)(2,1)}, u32[]{:S(2)}, u32[]{:S(2)}) collective-permute-start(bf16[1,320,1024]{2,1,0:T(8,128)(2,1)S(1)} %fusion.63), channel_id=1, source_target_pairs={{0,1},{1,2},{2,3},{3,4},{4,5},{5,6},{6,7},{7,8},{8,9},{9,10},{10,1... | collective-permute-start | bytes 1966088 | tf_op jit(solution)/shard_map/ppermute | solution.py:16
  277.5 9.7 %collective-permute-start.18 = (bf16[1,320,1024]{2,1,0:T(8,128)(2,1)}, bf16[1,320,1024]{2,1,0:T(8,128)(2,1)S(1)}, u32[]{:S(2)}, u32[]{:S(2)}) collective-permute-start(bf16[1,320,1024]{2,1,0:T(8,128)(2,1)} %fusion.44), channel_id=1, source_target_pairs={{0,64},{64,128},{128,192},{1,65},{65,129},{129,193},{2,66},{66,130... | collective-permute-start | bytes 1966088 | tf_op jit(solution)/shard_map/ppermute | solution.py:28
  279.4 21.3 %collective-permute-start.21 = (bf16[1,320,1024]{2,1,0:T(8,128)(2,1)S(1)}, bf16[1,320,1024]{2,1,0:T(8,128)(2,1)S(1)}, u32[]{:S(2)}, u32[]{:S(2)}) collective-permute-start(bf16[1,320,1024]{2,1,0:T(8,128)(2,1)S(1)} %get-tuple-element.15), channel_id=1, source_target_pairs={{0,64},{64,128},{128,192},{1,65},{65,129},{129,193},{2,66},{66,130... | collective-permute-start | bytes 1966088 | tf_op jit(solution)/shard_map/ppermute | solution.py:28
  287.6 27.2 %collective-permute-start.20 = (bf16[1,320,1024]{2,1,0:T(8,128)(2,1)S(1)}, bf16[1,320,1024]{2,1,0:T(8,128)(2,1)S(1)}, u32[]{:S(2)}, u32[]{:S(2)}) collective-permute-start(bf16[1,320,1024]{2,1,0:T(8,128)(2,1)S(1)} %fusion.66), channel_id=1, source_target_pairs={{1,0},{2,1},{3,2},{4,3},{5,4},{6,5},{7,6},{8,7},{9,8},{10,9},{11,1... | collective-permute-start | bytes 1966088 | tf_op jit(solution)/shard_map/ppermute | solution.py:18
  289.0 27.5 %collective-permute-start.19 = (bf16[1,320,1024]{2,1,0:T(8,128)(2,1)S(1)}, bf16[1,320,1024]{2,1,0:T(8,128)(2,1)}, u32[]{:S(2)}, u32[]{:S(2)}) collective-permute-start(bf16[1,320,1024]{2,1,0:T(8,128)(2,1)S(1)} %fusion.66), channel_id=1, source_target_pairs={{0,1},{1,2},{2,3},{3,4},{4,5},{5,6},{6,7},{7,8},{8,9},{9,10},{10,1... | collective-permute-start | bytes 1966088 | tf_op jit(solution)/shard_map/ppermute | solution.py:16
  320.0 35.2 %copy-start.3 = (bf16[1,320,1024]{2,1,0:T(8,128)(2,1)}, bf16[1,320,1024]{2,1,0:T(8,128)(2,1)S(1)}, u32[]{:S(2)}) copy-start(bf16[1,320,1024]{2,1,0:T(8,128)(2,1)S(1)} %fusion.43) | copy-start | bytes 1966084
  320.0 14.5 %collective-permute-start.22 = (bf16[1,320,1024]{2,1,0:T(8,128)(2,1)S(1)}, bf16[1,320,1024]{2,1,0:T(8,128)(2,1)S(1)}, u32[]{:S(2)}, u32[]{:S(2)}) collective-permute-start(bf16[1,320,1024]{2,1,0:T(8,128)(2,1)S(1)} %fusion.43), channel_id=1, source_target_pairs={{0,64},{64,128},{128,192},{1,65},{65,129},{129,193},{2,66},{66,130... | collective-permute-start | bytes 1966088 | tf_op jit(solution)/shard_map/ppermute | solution.py:28
  321.9 33.2 %collective-permute-start.25 = (bf16[1,320,1024]{2,1,0:T(8,128)(2,1)S(1)}, bf16[1,320,1024]{2,1,0:T(8,128)(2,1)S(1)}, u32[]{:S(2)}, u32[]{:S(2)}) collective-permute-start(bf16[1,320,1024]{2,1,0:T(8,128)(2,1)S(1)} %get-tuple-element.13), channel_id=1, source_target_pairs={{0,64},{64,128},{128,192},{1,65},{65,129},{129,193},{2,66},{66,130... | collective-permute-start | bytes 1966088 | tf_op jit(solution)/shard_map/ppermute | solution.py:28
  334.9 34.6 %collective-permute-start.24 = (bf16[1,320,1024]{2,1,0:T(8,128)(2,1)S(1)}, bf16[1,320,1024]{2,1,0:T(8,128)(2,1)S(1)}, u32[]{:S(2)}, u32[]{:S(2)}) collective-permute-start(bf16[1,320,1024]{2,1,0:T(8,128)(2,1)S(1)} %fusion.69), channel_id=1, source_target_pairs={{1,0},{2,1},{3,2},{4,3},{5,4},{6,5},{7,6},{8,7},{9,8},{10,9},{11,1... | collective-permute-start | bytes 1966088 | tf_op jit(solution)/shard_map/ppermute | solution.py:18
  336.2 40.1 %collective-permute-start.23 = (bf16[1,320,1024]{2,1,0:T(8,128)(2,1)S(1)}, bf16[1,320,1024]{2,1,0:T(8,128)(2,1)}, u32[]{:S(2)}, u32[]{:S(2)}) collective-permute-start(bf16[1,320,1024]{2,1,0:T(8,128)(2,1)S(1)} %fusion.69), channel_id=1, source_target_pairs={{0,1},{1,2},{2,3},{3,4},{4,5},{5,6},{6,7},{7,8},{8,9},{9,10},{10,1... | collective-permute-start | bytes 1966088 | tf_op jit(solution)/shard_map/ppermute | solution.py:16
  (1 other events, 3.9 us)
Sparse Core Ops, SparseCore 0:
  9.2 36.3 all-gather.1
  383.5 62.9 reduce-scatter.1
where the time goes:
time: 455 us; the launch traced here: 453 us
  waiting for transfers between devices  270 us (59%)
  starting transfers between devices  95.6 us (21%)
  matrix products  60.9 us (13%)
  between operations  13.9 us (3%)
  other arithmetic  12.4 us (3%)
    ppermute x12, waiting for transfers between devices, shifted(): return lax.ppermute(array, axis, pairs)  97.1 us
    reduce_scatter x1, waiting for transfers between devices, shards(): lax.psum_scatter(stacked.astype(jnp.bfloat16), 'segment', scatter_dimensi...  63.1 us
    ppermute x7, starting transfers between devices, extended(): lax.ppermute(tail, axis, [(i, (i + 1) % count) for i in range(ends)])  61.4 us
    dot_general x28, matrix products, channel_mix(): jnp.einsum('io,fip->fop', weight, field, preferred_element_type=jnp.float32)  60.7 us
    ppermute x7, waiting for transfers between devices, extended(): lax.ppermute(tail, axis, [(i, (i + 1) % count) for i in range(ends)])  42.2 us
    all_gather x1, waiting for transfers between devices, shards(): all_clips = lax.all_gather(clips, 'segment', axis=0, tiled=True)  35.6 us
    ppermute x7, waiting for transfers between devices, extended(): lax.ppermute(head, axis, [((i + 1) % count, i) for i in range(ends)])  31.1 us
    ppermute x12, starting transfers between devices, shifted(): return lax.ppermute(array, axis, pairs)  25.2 us
  transfers between devices with their start and end apart: 28, of which 22 were waited for; matrix products, arithmetic and copies ran while one was open for 10% of the time, Pallas kernels for 0%

commit v1 on v0

--- a/solution.py
+++ b/solution.py
@@ -61,7 +61,10 @@
     sections = lax.axis_size("segment")
     section = lax.axis_index("segment")
     emb = embed(timesteps, clips.shape[2])
-    all_clips = lax.all_gather(clips, "segment", axis=0, tiled=True)
+    size = lax.axis_size("segment")
+    blocks = jnp.stack([clips for _ in range(size)])
+    blocks = lax.all_to_all(blocks, "segment", split_axis=0, concat_axis=0)
+    all_clips = jnp.concatenate(blocks, axis=0)
     batches = all_clips.shape[0]
     film_all = jnp.dot(emb, film_weight[0], preferred_element_type=jnp.float32)
     own_gain = lax.dynamic_index_in_dim(gain, section, 0, keepdims=False)

time: 455 us -> 459 us (level)
  starting transfers between devices: 95.6 us -> 103 us
    all_gather x1 -> x0, waiting for transfers between devices: 35.6 us -> none  [shards(): all_clips = lax.all_gather(clips, 'segment', axis=0, tiled=True)]
    all_to_all x0 -> x1, waiting for transfers between devices: none -> 31.1 us  [shards(): blocks = lax.all_to_all(blocks, 'segment', split_axis=0, concat_axis=0)]
    all_to_all x0 -> x1, starting transfers between devices: none -> 7.88 us  [shards(): blocks = lax.all_to_all(blocks, 'segment', split_axis=0, concat_axis=0)]
    reduce_scatter x1, waiting for transfers between devices: 63.1 us -> 70.3 us  [shards(): lax.psum_scatter(stacked.astype(jnp.bfloat16), 'segment', scatter_dimensi...]
    ppermute x7, waiting for transfers between devices: 42.2 us -> 37 us  [extended(): lax.ppermute(tail, axis, [(i, (i + 1) % count) for i in range(ends)])]
  transfers between devices with their start and end apart: 28 -> 28, of which waited for: 22 -> 21; matrix products, arithmetic and copies ran while one was open for 10% -> 9% of each run, Pallas kernels for 0% -> 0%
where the time goes in v1:
time: 459 us; the launch traced here: 458 us
  waiting for transfers between devices  266 us (58%)
  starting transfers between devices  103 us (22%)
  matrix products  60.8 us (13%)
  between operations  13.9 us (3%)
  other arithmetic  10.7 us (2%)
    ppermute x12, waiting for transfers between devices, shifted(): return lax.ppermute(array, axis, pairs)  97.2 us
    reduce_scatter x1, waiting for transfers between devices, shards(): lax.psum_scatter(stacked.astype(jnp.bfloat16), 'segment', scatter_dimensi...  70.3 us
    ppermute x7, starting transfers between devices, extended(): lax.ppermute(tail, axis, [(i, (i + 1) % count) for i in range(ends)])  61.5 us
    dot_general x28, matrix products, channel_mix(): jnp.einsum('io,fip->fop', weight, field, preferred_element_type=jnp.float32)  60.6 us
    ppermute x7, waiting for transfers between devices, extended(): lax.ppermute(tail, axis, [(i, (i + 1) % count) for i in range(ends)])  37 us
    all_to_all x1, waiting for transfers between devices, shards(): blocks = lax.all_to_all(blocks, 'segment', split_axis=0, concat_axis=0)  31.1 us
    ppermute x7, waiting for transfers between devices, extended(): lax.ppermute(head, axis, [((i + 1) % count, i) for i in range(ends)])  30.4 us
    ppermute x12, starting transfers between devices, shifted(): return lax.ppermute(array, axis, pairs)  24.3 us
  transfers between devices with their start and end apart: 28, of which 21 were waited for; matrix products, arithmetic and copies ran while one was open for 9% of the time, Pallas kernels for 0%

profile of v1, /device:TPU:1, one launch (start us, length us, event | category | flops | bytes accessed | tf_op | source)
XLA Modules:
  0.0 457.8 jit_solution(9121674600165378628)
XLA Ops:
  9.5 7.9 %all-to-all-start = ((bf16[4,1,1,320,1024]{4,3,2,1,0:T(8,128)(2,1)}), bf16[4,1,1,320,1024]{4,3,2,1,0:T(8,128)(2,1)}, u32[]{:S(2)}, u32[]{:S(2)}) async-start(bf16[4,1,1,320,1024]{4,3,2,1,0:T(8,128)(2,1)} %stack.22), calls=%async_computation | async-start | bytes 5242880 | tf_op jit(solution)/shard_map/all_to_all | solution.py:66
  18.4 31.1 %all-to-all-done = bf16[4,1,1,320,1024]{4,3,2,1,0:T(8,128)(2,1)} async-done(((bf16[4,1,1,320,1024]{4,3,2,1,0:T(8,128)(2,1)}), bf16[4,1,1,320,1024]{4,3,2,1,0:T(8,128)(2,1)}, u32[]{:S(2)}, u32[]{:S(2)}) %all-to-all-start) | async-done | bytes 2621472 | tf_op jit(solution)/shard_map/all_to_all | solution.py:66
  52.5 4.9 %collective-permute-start = (bf16[1,320,1024]{2,1,0:T(8,128)(2,1)S(1)}, bf16[1,320,1024]{2,1,0:T(8,128)(2,1)}, u32[]{:S(2)}, u32[]{:S(2)}) collective-permute-start(bf16[1,320,1024]{2,1,0:T(8,128)(2,1)S(1)} %fusion.51), channel_id=1, source_target_pairs={{0,1},{1,2},{2,3},{3,4},{4,5},{5,6},{6,7},{7,8},{8,9},{9,10},{10,1... | collective-permute-start | bytes 1966088 | tf_op jit(solution)/shard_map/ppermute | solution.py:16
  60.2 8.1 %collective-permute-done.1 = bf16[1,320,1024]{2,1,0:T(8,128)(2,1)S(1)} collective-permute-done((bf16[1,320,1024]{2,1,0:T(8,128)(2,1)S(1)}, bf16[1,320,1024]{2,1,0:T(8,128)(2,1)S(1)}, u32[]{:S(2)}, u32[]{:S(2)}) %collective-permute-start.1) | collective-permute-done | bytes 655392 | tf_op jit(solution)/shard_map/ppermute | solution.py:18
  69.9 12.0 %collective-permute-done = bf16[1,320,1024]{2,1,0:T(8,128)(2,1)} collective-permute-done((bf16[1,320,1024]{2,1,0:T(8,128)(2,1)S(1)}, bf16[1,320,1024]{2,1,0:T(8,128)(2,1)}, u32[]{:S(2)}, u32[]{:S(2)}) %collective-permute-start) | collective-permute-done | bytes 655392 | tf_op jit(solution)/shard_map/ppermute | solution.py:16
  90.6 5.6 %collective-permute-done.2 = bf16[1,320,1024]{2,1,0:T(8,128)(2,1)S(1)} collective-permute-done((bf16[1,320,1024]{2,1,0:T(8,128)(2,1)S(1)}, bf16[1,320,1024]{2,1,0:T(8,128)(2,1)S(1)}, u32[]{:S(2)}, u32[]{:S(2)}) %collective-permute-start.2) | collective-permute-done | bytes 655392 | tf_op jit(solution)/shard_map/ppermute | solution.py:28
  99.0 5.9 %collective-permute-start.3 = (bf16[1,320,1024]{2,1,0:T(8,128)(2,1)S(1)}, bf16[1,320,1024]{2,1,0:T(8,128)(2,1)}, u32[]{:S(2)}, u32[]{:S(2)}) collective-permute-start(bf16[1,320,1024]{2,1,0:T(8,128)(2,1)S(1)} %fusion.54), channel_id=1, source_target_pairs={{0,1},{1,2},{2,3},{3,4},{4,5},{5,6},{6,7},{7,8},{8,9},{9,10},{10,1... | collective-permute-start | bytes 1966088 | tf_op jit(solution)/shard_map/ppermute | solution.py:16
  104.9 17.2 %collective-permute-done.5 = bf16[1,320,1024]{2,1,0:T(8,128)(2,1)S(1)} collective-permute-done((bf16[1,320,1024]{2,1,0:T(8,128)(2,1)S(1)}, bf16[1,320,1024]{2,1,0:T(8,128)(2,1)S(1)}, u32[]{:S(2)}, u32[]{:S(2)}) %collective-permute-start.5) | collective-permute-done | bytes 655392 | tf_op jit(solution)/shard_map/ppermute | solution.py:28
  127.0 4.3 collective-permute-done.3
  138.6 5.6 %collective-permute-done.6 = bf16[1,320,1024]{2,1,0:T(8,128)(2,1)S(1)} collective-permute-done((bf16[1,320,1024]{2,1,0:T(8,128)(2,1)S(1)}, bf16[1,320,1024]{2,1,0:T(8,128)(2,1)S(1)}, u32[]{:S(2)}, u32[]{:S(2)}) %collective-permute-start.6) | collective-permute-done | bytes 655392 | tf_op jit(solution)/shard_map/ppermute | solution.py:28
  147.0 6.2 %collective-permute-start.7 = (bf16[1,320,1024]{2,1,0:T(8,128)(2,1)S(1)}, bf16[1,320,1024]{2,1,0:T(8,128)(2,1)}, u32[]{:S(2)}, u32[]{:S(2)}) collective-permute-start(bf16[1,320,1024]{2,1,0:T(8,128)(2,1)S(1)} %fusion.57), channel_id=1, source_target_pairs={{0,1},{1,2},{2,3},{3,4},{4,5},{5,6},{6,7},{7,8},{8,9},{9,10},{10,1... | collective-permute-start | bytes 1966088 | tf_op jit(solution)/shard_map/ppermute | solution.py:16
  153.2 15.6 %collective-permute-done.9 = bf16[1,320,1024]{2,1,0:T(8,128)(2,1)S(1)} collective-permute-done((bf16[1,320,1024]{2,1,0:T(8,128)(2,1)S(1)}, bf16[1,320,1024]{2,1,0:T(8,128)(2,1)S(1)}, u32[]{:S(2)}, u32[]{:S(2)}) %collective-permute-start.9) | collective-permute-done | bytes 655392 | tf_op jit(solution)/shard_map/ppermute | solution.py:28
  172.7 6.6 %collective-permute-done.7 = bf16[1,320,1024]{2,1,0:T(8,128)(2,1)} collective-permute-done((bf16[1,320,1024]{2,1,0:T(8,128)(2,1)S(1)}, bf16[1,320,1024]{2,1,0:T(8,128)(2,1)}, u32[]{:S(2)}, u32[]{:S(2)}) %collective-permute-start.7) | collective-permute-done | bytes 655392 | tf_op jit(solution)/shard_map/ppermute | solution.py:16
  179.3 3.9 fusion.46
  187.0 5.9 %collective-permute-done.10 = bf16[1,320,1024]{2,1,0:T(8,128)(2,1)S(1)} collective-permute-done((bf16[1,320,1024]{2,1,0:T(8,128)(2,1)}, bf16[1,320,1024]{2,1,0:T(8,128)(2,1)S(1)}, u32[]{:S(2)}, u32[]{:S(2)}) %collective-permute-start.10) | collective-permute-done | bytes 655392 | tf_op jit(solution)/shard_map/ppermute | solution.py:28
  195.8 6.4 %collective-permute-start.11 = (bf16[1,320,1024]{2,1,0:T(8,128)(2,1)S(1)}, bf16[1,320,1024]{2,1,0:T(8,128)(2,1)}, u32[]{:S(2)}, u32[]{:S(2)}) collective-permute-start(bf16[1,320,1024]{2,1,0:T(8,128)(2,1)S(1)} %fusion.60), channel_id=1, source_target_pairs={{0,1},{1,2},{2,3},{3,4},{4,5},{5,6},{6,7},{7,8},{8,9},{9,10},{10,1... | collective-permute-start | bytes 1966088 | tf_op jit(solution)/shard_map/ppermute | solution.py:16
  202.2 15.5 %collective-permute-done.13 = bf16[1,320,1024]{2,1,0:T(8,128)(2,1)S(1)} collective-permute-done((bf16[1,320,1024]{2,1,0:T(8,128)(2,1)S(1)}, bf16[1,320,1024]{2,1,0:T(8,128)(2,1)S(1)}, u32[]{:S(2)}, u32[]{:S(2)}) %collective-permute-start.13) | collective-permute-done | bytes 655392 | tf_op jit(solution)/shard_map/ppermute | solution.py:28
  223.7 4.2 collective-permute-done.11
  227.9 3.5 fusion.45
  235.3 5.6 %collective-permute-done.14 = bf16[1,320,1024]{2,1,0:T(8,128)(2,1)S(1)} collective-permute-done((bf16[1,320,1024]{2,1,0:T(8,128)(2,1)S(1)}, bf16[1,320,1024]{2,1,0:T(8,128)(2,1)S(1)}, u32[]{:S(2)}, u32[]{:S(2)}) %collective-permute-start.14) | collective-permute-done | bytes 655392 | tf_op jit(solution)/shard_map/ppermute | solution.py:28
  242.6 7.3 %collective-permute-start.15 = (bf16[1,320,1024]{2,1,0:T(8,128)(2,1)S(1)}, bf16[1,320,1024]{2,1,0:T(8,128)(2,1)}, u32[]{:S(2)}, u32[]{:S(2)}) collective-permute-start(bf16[1,320,1024]{2,1,0:T(8,128)(2,1)S(1)} %fusion.63), channel_id=1, source_target_pairs={{0,1},{1,2},{2,3},{3,4},{4,5},{5,6},{6,7},{7,8},{8,9},{9,10},{10,1... | collective-permute-start | bytes 1966088 | tf_op jit(solution)/shard_map/ppermute | solution.py:16
  249.9 9.7 %collective-permute-done.17 = bf16[1,320,1024]{2,1,0:T(8,128)(2,1)S(1)} collective-permute-done((bf16[1,320,1024]{2,1,0:T(8,128)(2,1)S(1)}, bf16[1,320,1024]{2,1,0:T(8,128)(2,1)S(1)}, u32[]{:S(2)}, u32[]{:S(2)}) %collective-permute-start.17) | collective-permute-done | bytes 655392 | tf_op jit(solution)/shard_map/ppermute | solution.py:28
  266.0 10.0 %collective-permute-done.15 = bf16[1,320,1024]{2,1,0:T(8,128)(2,1)} collective-permute-done((bf16[1,320,1024]{2,1,0:T(8,128)(2,1)S(1)}, bf16[1,320,1024]{2,1,0:T(8,128)(2,1)}, u32[]{:S(2)}, u32[]{:S(2)}) %collective-permute-start.15) | collective-permute-done | bytes 655392 | tf_op jit(solution)/shard_map/ppermute | solution.py:16
  275.9 3.9 fusion.44
  283.7 5.9 %collective-permute-done.18 = bf16[1,320,1024]{2,1,0:T(8,128)(2,1)S(1)} collective-permute-done((bf16[1,320,1024]{2,1,0:T(8,128)(2,1)}, bf16[1,320,1024]{2,1,0:T(8,128)(2,1)S(1)}, u32[]{:S(2)}, u32[]{:S(2)}) %collective-permute-start.18) | collective-permute-done | bytes 655392 | tf_op jit(solution)/shard_map/ppermute | solution.py:28
  291.3 12.0 %collective-permute-start.19 = (bf16[1,320,1024]{2,1,0:T(8,128)(2,1)S(1)}, bf16[1,320,1024]{2,1,0:T(8,128)(2,1)}, u32[]{:S(2)}, u32[]{:S(2)}) collective-permute-start(bf16[1,320,1024]{2,1,0:T(8,128)(2,1)S(1)} %fusion.66), channel_id=1, source_target_pairs={{0,1},{1,2},{2,3},{3,4},{4,5},{5,6},{6,7},{7,8},{8,9},{9,10},{10,1... | collective-permute-start | bytes 1966088 | tf_op jit(solution)/shard_map/ppermute | solution.py:16
  307.7 9.7 %collective-permute-done.20 = bf16[1,320,1024]{2,1,0:T(8,128)(2,1)S(1)} collective-permute-done((bf16[1,320,1024]{2,1,0:T(8,128)(2,1)S(1)}, bf16[1,320,1024]{2,1,0:T(8,128)(2,1)S(1)}, u32[]{:S(2)}, u32[]{:S(2)}) %collective-permute-start.20) | collective-permute-done | bytes 655392 | tf_op jit(solution)/shard_map/ppermute | solution.py:18
  326.4 10.7 %collective-permute-done.22 = bf16[1,320,1024]{2,1,0:T(8,128)(2,1)S(1)} collective-permute-done((bf16[1,320,1024]{2,1,0:T(8,128)(2,1)S(1)}, bf16[1,320,1024]{2,1,0:T(8,128)(2,1)S(1)}, u32[]{:S(2)}, u32[]{:S(2)}) %collective-permute-start.22) | collective-permute-done | bytes 655392 | tf_op jit(solution)/shard_map/ppermute | solution.py:28
  338.8 18.9 %collective-permute-start.23 = (bf16[1,320,1024]{2,1,0:T(8,128)(2,1)S(1)}, bf16[1,320,1024]{2,1,0:T(8,128)(2,1)}, u32[]{:S(2)}, u32[]{:S(2)}) collective-permute-start(bf16[1,320,1024]{2,1,0:T(8,128)(2,1)S(1)} %fusion.69), channel_id=1, source_target_pairs={{0,1},{1,2},{2,3},{3,4},{4,5},{5,6},{6,7},{7,8},{8,9},{9,10},{10,1... | collective-permute-start | bytes 1966088 | tf_op jit(solution)/shard_map/ppermute | solution.py:16
  361.0 11.1 %collective-permute-done.24 = bf16[1,320,1024]{2,1,0:T(8,128)(2,1)S(1)} collective-permute-done((bf16[1,320,1024]{2,1,0:T(8,128)(2,1)S(1)}, bf16[1,320,1024]{2,1,0:T(8,128)(2,1)S(1)}, u32[]{:S(2)}, u32[]{:S(2)}) %collective-permute-start.24) | collective-permute-done | bytes 655392 | tf_op jit(solution)/shard_map/ppermute | solution.py:18
  373.7 3.9 fusion.72
  380.7 70.3 %reduce-scatter.2.cloned.1.call-done = bf16[1,1,320,1024]{3,2,1,0:T(8,128)(2,1)} async-done(((bf16[4,1,320,1024]{3,2,1,0:T(8,128)(2,1)}), bf16[1,1,320,1024]{3,2,1,0:T(8,128)(2,1)}) %reduce-scatter.2.cloned.1.call-update) | async-done | bytes 655376 | tf_op jit(solution)/shard_map/reduce_scatter | solution.py:101
  (107 shorter events, 94.9 us)
Async XLA Ops:
  6.5 75.3 %copy-start = (bf16[1,320,320]{2,1,0:T(8,128)(2,1)S(1)}, bf16[1,320,320]{2,1,0:T(8,128)(2,1)}, u32[]{:S(2)}) copy-start(bf16[1,320,320]{2,1,0:T(8,128)(2,1)} %param.12) | copy-start | bytes 614404
  9.5 39.9 %all-to-all-start = ((bf16[4,1,1,320,1024]{4,3,2,1,0:T(8,128)(2,1)}), bf16[4,1,1,320,1024]{4,3,2,1,0:T(8,128)(2,1)}, u32[]{:S(2)}, u32[]{:S(2)}) async-start(bf16[4,1,1,320,1024]{4,3,2,1,0:T(8,128)(2,1)} %stack.22), calls=%async_computation | async-start | bytes 5242880 | tf_op jit(solution)/shard_map/all_to_all | solution.py:66
  17.4 433.6 %reduce-scatter.2.cloned.1.call-start = ((), (), s32[]{:S(2)}) async-start(), calls=%async_computation.2 | async-start | bytes 3276800 | tf_op jit(solution)/shard_map/reduce_scatter | solution.py:101
  18.4 33.9 %copy-start.5 = (bf16[1,320,320]{2,1,0:T(8,128)(2,1)S(1)}, bf16[1,320,320]{2,1,0:T(8,128)(2,1)}, u32[]{:S(2)}) copy-start(bf16[1,320,320]{2,1,0:T(8,128)(2,1)} %param.11) | copy-start | bytes 614404
  18.4 39.0 %copy-start.1 = (bf16[1,3,320,320]{3,2,1,0:T(8,128)(2,1)S(1)}, bf16[1,3,320,320]{3,2,1,0:T(8,128)(2,1)}, u32[]{:S(2)}) copy-start(bf16[1,3,320,320]{3,2,1,0:T(8,128)(2,1)} %param.10) | copy-start | bytes 1843204
  51.0 17.3 %collective-permute-start.1 = (bf16[1,320,1024]{2,1,0:T(8,128)(2,1)S(1)}, bf16[1,320,1024]{2,1,0:T(8,128)(2,1)S(1)}, u32[]{:S(2)}, u32[]{:S(2)}) collective-permute-start(bf16[1,320,1024]{2,1,0:T(8,128)(2,1)S(1)} %fusion.51), channel_id=1, source_target_pairs={{1,0},{2,1},{3,2},{4,3},{5,4},{6,5},{7,6},{8,7},{9,8},{10,9},{11,1... | collective-permute-start | bytes 1966088 | tf_op jit(solution)/shard_map/ppermute | solution.py:18
  52.5 29.3 %collective-permute-start = (bf16[1,320,1024]{2,1,0:T(8,128)(2,1)S(1)}, bf16[1,320,1024]{2,1,0:T(8,128)(2,1)}, u32[]{:S(2)}, u32[]{:S(2)}) collective-permute-start(bf16[1,320,1024]{2,1,0:T(8,128)(2,1)S(1)} %fusion.51), channel_id=1, source_target_pairs={{0,1},{1,2},{2,3},{3,4},{4,5},{5,6},{6,7},{7,8},{8,9},{9,10},{10,1... | collective-permute-start | bytes 1966088 | tf_op jit(solution)/shard_map/ppermute | solution.py:16
  85.4 10.8 %collective-permute-start.2 = (bf16[1,320,1024]{2,1,0:T(8,128)(2,1)S(1)}, bf16[1,320,1024]{2,1,0:T(8,128)(2,1)S(1)}, u32[]{:S(2)}, u32[]{:S(2)}) collective-permute-start(bf16[1,320,1024]{2,1,0:T(8,128)(2,1)S(1)} %fusion.48), channel_id=1, source_target_pairs={{0,64},{64,128},{128,192},{1,65},{65,129},{129,193},{2,66},{66,130... | collective-permute-start | bytes 1966088 | tf_op jit(solution)/shard_map/ppermute | solution.py:28
  88.6 33.4 %collective-permute-start.5 = (bf16[1,320,1024]{2,1,0:T(8,128)(2,1)S(1)}, bf16[1,320,1024]{2,1,0:T(8,128)(2,1)S(1)}, u32[]{:S(2)}, u32[]{:S(2)}) collective-permute-start(bf16[1,320,1024]{2,1,0:T(8,128)(2,1)S(1)} %get-tuple-element.23), channel_id=1, source_target_pairs={{0,64},{64,128},{128,192},{1,65},{65,129},{129,193},{2,66},{66,130... | collective-permute-start | bytes 1966088 | tf_op jit(solution)/shard_map/ppermute | solution.py:28
  97.7 27.6 %collective-permute-start.4 = (bf16[1,320,1024]{2,1,0:T(8,128)(2,1)S(1)}, bf16[1,320,1024]{2,1,0:T(8,128)(2,1)S(1)}, u32[]{:S(2)}, u32[]{:S(2)}) collective-permute-start(bf16[1,320,1024]{2,1,0:T(8,128)(2,1)S(1)} %fusion.54), channel_id=1, source_target_pairs={{1,0},{2,1},{3,2},{4,3},{5,4},{6,5},{7,6},{8,7},{9,8},{10,9},{11,1... | collective-permute-start | bytes 1966088 | tf_op jit(solution)/shard_map/ppermute | solution.py:18
  99.0 32.2 %collective-permute-start.3 = (bf16[1,320,1024]{2,1,0:T(8,128)(2,1)S(1)}, bf16[1,320,1024]{2,1,0:T(8,128)(2,1)}, u32[]{:S(2)}, u32[]{:S(2)}) collective-permute-start(bf16[1,320,1024]{2,1,0:T(8,128)(2,1)S(1)} %fusion.54), channel_id=1, source_target_pairs={{0,1},{1,2},{2,3},{3,4},{4,5},{5,6},{6,7},{7,8},{8,9},{9,10},{10,1... | collective-permute-start | bytes 1966088 | tf_op jit(solution)/shard_map/ppermute | solution.py:16
  134.7 9.4 %collective-permute-start.6 = (bf16[1,320,1024]{2,1,0:T(8,128)(2,1)S(1)}, bf16[1,320,1024]{2,1,0:T(8,128)(2,1)S(1)}, u32[]{:S(2)}, u32[]{:S(2)}) collective-permute-start(bf16[1,320,1024]{2,1,0:T(8,128)(2,1)S(1)} %fusion.47), channel_id=1, source_target_pairs={{0,64},{64,128},{128,192},{1,65},{65,129},{129,193},{2,66},{66,130... | collective-permute-start | bytes 1966088 | tf_op jit(solution)/shard_map/ppermute | solution.py:28
  136.6 32.2 %collective-permute-start.9 = (bf16[1,320,1024]{2,1,0:T(8,128)(2,1)S(1)}, bf16[1,320,1024]{2,1,0:T(8,128)(2,1)S(1)}, u32[]{:S(2)}, u32[]{:S(2)}) collective-permute-start(bf16[1,320,1024]{2,1,0:T(8,128)(2,1)S(1)} %get-tuple-element.21), channel_id=1, source_target_pairs={{0,64},{64,128},{128,192},{1,65},{65,129},{129,193},{2,66},{66,130... | collective-permute-start | bytes 1966088 | tf_op jit(solution)/shard_map/ppermute | solution.py:28
  145.7 25.3 %collective-permute-start.8 = (bf16[1,320,1024]{2,1,0:T(8,128)(2,1)S(1)}, bf16[1,320,1024]{2,1,0:T(8,128)(2,1)S(1)}, u32[]{:S(2)}, u32[]{:S(2)}) collective-permute-start(bf16[1,320,1024]{2,1,0:T(8,128)(2,1)S(1)} %fusion.57), channel_id=1, source_target_pairs={{1,0},{2,1},{3,2},{4,3},{5,4},{6,5},{7,6},{8,7},{9,8},{10,9},{11,1... | collective-permute-start | bytes 1966088 | tf_op jit(solution)/shard_map/ppermute | solution.py:18
  147.0 32.2 %collective-permute-start.7 = (bf16[1,320,1024]{2,1,0:T(8,128)(2,1)S(1)}, bf16[1,320,1024]{2,1,0:T(8,128)(2,1)}, u32[]{:S(2)}, u32[]{:S(2)}) collective-permute-start(bf16[1,320,1024]{2,1,0:T(8,128)(2,1)S(1)} %fusion.57), channel_id=1, source_target_pairs={{0,1},{1,2},{2,3},{3,4},{4,5},{5,6},{6,7},{7,8},{8,9},{9,10},{10,1... | collective-permute-start | bytes 1966088 | tf_op jit(solution)/shard_map/ppermute | solution.py:16
  183.2 9.7 %collective-permute-start.10 = (bf16[1,320,1024]{2,1,0:T(8,128)(2,1)}, bf16[1,320,1024]{2,1,0:T(8,128)(2,1)S(1)}, u32[]{:S(2)}, u32[]{:S(2)}) collective-permute-start(bf16[1,320,1024]{2,1,0:T(8,128)(2,1)} %fusion.46), channel_id=1, source_target_pairs={{0,64},{64,128},{128,192},{1,65},{65,129},{129,193},{2,66},{66,130... | collective-permute-start | bytes 1966088 | tf_op jit(solution)/shard_map/ppermute | solution.py:28
  185.1 32.6 %collective-permute-start.13 = (bf16[1,320,1024]{2,1,0:T(8,128)(2,1)S(1)}, bf16[1,320,1024]{2,1,0:T(8,128)(2,1)S(1)}, u32[]{:S(2)}, u32[]{:S(2)}) collective-permute-start(bf16[1,320,1024]{2,1,0:T(8,128)(2,1)S(1)} %get-tuple-element.19), channel_id=1, source_target_pairs={{0,64},{64,128},{128,192},{1,65},{65,129},{129,193},{2,66},{66,130... | collective-permute-start | bytes 1966088 | tf_op jit(solution)/shard_map/ppermute | solution.py:28
  194.5 27.6 %collective-permute-start.12 = (bf16[1,320,1024]{2,1,0:T(8,128)(2,1)S(1)}, bf16[1,320,1024]{2,1,0:T(8,128)(2,1)S(1)}, u32[]{:S(2)}, u32[]{:S(2)}) collective-permute-start(bf16[1,320,1024]{2,1,0:T(8,128)(2,1)S(1)} %fusion.60), channel_id=1, source_target_pairs={{1,0},{2,1},{3,2},{4,3},{5,4},{6,5},{7,6},{8,7},{9,8},{10,9},{11,1... | collective-permute-start | bytes 1966088 | tf_op jit(solution)/shard_map/ppermute | solution.py:18
  195.8 32.1 %collective-permute-start.11 = (bf16[1,320,1024]{2,1,0:T(8,128)(2,1)S(1)}, bf16[1,320,1024]{2,1,0:T(8,128)(2,1)}, u32[]{:S(2)}, u32[]{:S(2)}) collective-permute-start(bf16[1,320,1024]{2,1,0:T(8,128)(2,1)S(1)} %fusion.60), channel_id=1, source_target_pairs={{0,1},{1,2},{2,3},{3,4},{4,5},{5,6},{6,7},{7,8},{8,9},{9,10},{10,1... | collective-permute-start | bytes 1966088 | tf_op jit(solution)/shard_map/ppermute | solution.py:16
  231.4 9.4 %collective-permute-start.14 = (bf16[1,320,1024]{2,1,0:T(8,128)(2,1)S(1)}, bf16[1,320,1024]{2,1,0:T(8,128)(2,1)S(1)}, u32[]{:S(2)}, u32[]{:S(2)}) collective-permute-start(bf16[1,320,1024]{2,1,0:T(8,128)(2,1)S(1)} %fusion.45), channel_id=1, source_target_pairs={{0,64},{64,128},{128,192},{1,65},{65,129},{129,193},{2,66},{66,130... | collective-permute-start | bytes 1966088 | tf_op jit(solution)/shard_map/ppermute | solution.py:28
  233.3 26.3 %collective-permute-start.17 = (bf16[1,320,1024]{2,1,0:T(8,128)(2,1)S(1)}, bf16[1,320,1024]{2,1,0:T(8,128)(2,1)S(1)}, u32[]{:S(2)}, u32[]{:S(2)}) collective-permute-start(bf16[1,320,1024]{2,1,0:T(8,128)(2,1)S(1)} %get-tuple-element.17), channel_id=1, source_target_pairs={{0,64},{64,128},{128,192},{1,65},{65,129},{129,193},{2,66},{66,130... | collective-permute-start | bytes 1966088 | tf_op jit(solution)/shard_map/ppermute | solution.py:28
  241.3 23.1 %collective-permute-start.16 = (bf16[1,320,1024]{2,1,0:T(8,128)(2,1)S(1)}, bf16[1,320,1024]{2,1,0:T(8,128)(2,1)S(1)}, u32[]{:S(2)}, u32[]{:S(2)}) collective-permute-start(bf16[1,320,1024]{2,1,0:T(8,128)(2,1)S(1)} %fusion.63), channel_id=1, source_target_pairs={{1,0},{2,1},{3,2},{4,3},{5,4},{6,5},{7,6},{8,7},{9,8},{10,9},{11,1... | collective-permute-start | bytes 1966088 | tf_op jit(solution)/shard_map/ppermute | solution.py:18
  242.6 33.4 %collective-permute-start.15 = (bf16[1,320,1024]{2,1,0:T(8,128)(2,1)S(1)}, bf16[1,320,1024]{2,1,0:T(8,128)(2,1)}, u32[]{:S(2)}, u32[]{:S(2)}) collective-permute-start(bf16[1,320,1024]{2,1,0:T(8,128)(2,1)S(1)} %fusion.63), channel_id=1, source_target_pairs={{0,1},{1,2},{2,3},{3,4},{4,5},{5,6},{6,7},{7,8},{8,9},{9,10},{10,1... | collective-permute-start | bytes 1966088 | tf_op jit(solution)/shard_map/ppermute | solution.py:16
  279.8 9.7 %collective-permute-start.18 = (bf16[1,320,1024]{2,1,0:T(8,128)(2,1)}, bf16[1,320,1024]{2,1,0:T(8,128)(2,1)S(1)}, u32[]{:S(2)}, u32[]{:S(2)}) collective-permute-start(bf16[1,320,1024]{2,1,0:T(8,128)(2,1)} %fusion.44), channel_id=1, source_target_pairs={{0,64},{64,128},{128,192},{1,65},{65,129},{129,193},{2,66},{66,130... | collective-permute-start | bytes 1966088 | tf_op jit(solution)/shard_map/ppermute | solution.py:28
  281.8 21.5 %collective-permute-start.21 = (bf16[1,320,1024]{2,1,0:T(8,128)(2,1)S(1)}, bf16[1,320,1024]{2,1,0:T(8,128)(2,1)S(1)}, u32[]{:S(2)}, u32[]{:S(2)}) collective-permute-start(bf16[1,320,1024]{2,1,0:T(8,128)(2,1)S(1)} %get-tuple-element.15), channel_id=1, source_target_pairs={{0,64},{64,128},{128,192},{1,65},{65,129},{129,193},{2,66},{66,130... | collective-permute-start | bytes 1966088 | tf_op jit(solution)/shard_map/ppermute | solution.py:28
  290.0 27.4 %collective-permute-start.20 = (bf16[1,320,1024]{2,1,0:T(8,128)(2,1)S(1)}, bf16[1,320,1024]{2,1,0:T(8,128)(2,1)S(1)}, u32[]{:S(2)}, u32[]{:S(2)}) collective-permute-start(bf16[1,320,1024]{2,1,0:T(8,128)(2,1)S(1)} %fusion.66), channel_id=1, source_target_pairs={{1,0},{2,1},{3,2},{4,3},{5,4},{6,5},{7,6},{8,7},{9,8},{10,9},{11,1... | collective-permute-start | bytes 1966088 | tf_op jit(solution)/shard_map/ppermute | solution.py:18
  291.3 27.7 %collective-permute-start.19 = (bf16[1,320,1024]{2,1,0:T(8,128)(2,1)S(1)}, bf16[1,320,1024]{2,1,0:T(8,128)(2,1)}, u32[]{:S(2)}, u32[]{:S(2)}) collective-permute-start(bf16[1,320,1024]{2,1,0:T(8,128)(2,1)S(1)} %fusion.66), channel_id=1, source_target_pairs={{0,1},{1,2},{2,3},{3,4},{4,5},{5,6},{6,7},{7,8},{8,9},{9,10},{10,1... | collective-permute-start | bytes 1966088 | tf_op jit(solution)/shard_map/ppermute | solution.py:16
  322.5 35.2 %copy-start.3 = (bf16[1,320,1024]{2,1,0:T(8,128)(2,1)}, bf16[1,320,1024]{2,1,0:T(8,128)(2,1)S(1)}, u32[]{:S(2)}) copy-start(bf16[1,320,1024]{2,1,0:T(8,128)(2,1)S(1)} %fusion.43) | copy-start | bytes 1966084
  322.5 14.5 %collective-permute-start.22 = (bf16[1,320,1024]{2,1,0:T(8,128)(2,1)S(1)}, bf16[1,320,1024]{2,1,0:T(8,128)(2,1)S(1)}, u32[]{:S(2)}, u32[]{:S(2)}) collective-permute-start(bf16[1,320,1024]{2,1,0:T(8,128)(2,1)S(1)} %fusion.43), channel_id=1, source_target_pairs={{0,64},{64,128},{128,192},{1,65},{65,129},{129,193},{2,66},{66,130... | collective-permute-start | bytes 1966088 | tf_op jit(solution)/shard_map/ppermute | solution.py:28
  324.4 33.3 %collective-permute-start.25 = (bf16[1,320,1024]{2,1,0:T(8,128)(2,1)S(1)}, bf16[1,320,1024]{2,1,0:T(8,128)(2,1)S(1)}, u32[]{:S(2)}, u32[]{:S(2)}) collective-permute-start(bf16[1,320,1024]{2,1,0:T(8,128)(2,1)S(1)} %get-tuple-element.13), channel_id=1, source_target_pairs={{0,64},{64,128},{128,192},{1,65},{65,129},{129,193},{2,66},{66,130... | collective-permute-start | bytes 1966088 | tf_op jit(solution)/shard_map/ppermute | solution.py:28
  337.5 34.6 %collective-permute-start.24 = (bf16[1,320,1024]{2,1,0:T(8,128)(2,1)S(1)}, bf16[1,320,1024]{2,1,0:T(8,128)(2,1)S(1)}, u32[]{:S(2)}, u32[]{:S(2)}) collective-permute-start(bf16[1,320,1024]{2,1,0:T(8,128)(2,1)S(1)} %fusion.69), channel_id=1, source_target_pairs={{1,0},{2,1},{3,2},{4,3},{5,4},{6,5},{7,6},{8,7},{9,8},{10,9},{11,1... | collective-permute-start | bytes 1966088 | tf_op jit(solution)/shard_map/ppermute | solution.py:18
  338.8 34.9 %collective-permute-start.23 = (bf16[1,320,1024]{2,1,0:T(8,128)(2,1)S(1)}, bf16[1,320,1024]{2,1,0:T(8,128)(2,1)}, u32[]{:S(2)}, u32[]{:S(2)}) collective-permute-start(bf16[1,320,1024]{2,1,0:T(8,128)(2,1)S(1)} %fusion.69), channel_id=1, source_target_pairs={{0,1},{1,2},{2,3},{3,4},{4,5},{5,6},{6,7},{7,8},{8,9},{9,10},{10,1... | collective-permute-start | bytes 1966088 | tf_op jit(solution)/shard_map/ppermute | solution.py:16
  (3 other events, 20.5 us)
Sparse Core Ops, SparseCore 0:
  380.9 70.0 reduce-scatter.1
